TPU v7x, 32 devices: a whole 2x2x4 slice. The times are simulated.
32 devices in a mesh: grp: 2 (over x), tp: 16 (over z, y, core).
Axes of the slice: x: 2, y: 2, z: 4, core: 2. Of those that a mesh axis runs over, the one named last changes fastest.
Arguments:
- tokens: bfloat16 [8192, 256], P('tp', 'grp'), parts along dimension 1, may hold values from -400 to 400
- norm_gain: bfloat16 [8192], P('tp'), may hold values from 0.099609375 to 1.8984375
- gate_weight: bfloat16 [8192, 28672], P(None, 'tp'), may hold values from -0.0625 to 0.0625
- up_weight: bfloat16 [8192, 28672], P(None, 'tp'), may hold values from -0.0625 to 0.0625
- down_weight: bfloat16 [28672, 8192], P('tp'), may hold values from -0.046875 to 0.046875
- target: bfloat16 [8192, 256], P('tp', 'grp'), parts along dimension 1, may hold values from -6 to 6
- probe_seeds: int32 [4], P('grp'), parts along dimension 0, may hold values from 0 to 1073741823
Outputs:
- unit_traces: float32 [6, 28672], P('grp', 'tp'), parts along dimension 0
There are 2 independent parts, one for each index of `grp`. A program takes and returns all parts, laid end to end along the dimension named above; an argument that names none is the same for every part. Nothing has to cross between parts.
All inputs are finite; a program needn't handle non-finite values.
Results may differ from a plain program's by a relative error of at most 0.0029.
Values may be sent and summed in bfloat16 or wider, within the bound.
A program may use at most 256 MiB of HBM per device.

v0:
```python
import jax
import jax.numpy as jnp
from jax import lax
from jax.sharding import PartitionSpec as P

D = 8192
FF = 28672


EPSILON = 1e-05
LEADING = (((0,), (0,)), ((), ()))


def mixing(mixed_word):
    mixed_word = mixed_word ^ lax.shift_right_logical(mixed_word, jnp.int32(16))
    mixed_word = mixed_word * jnp.int32(73244475)
    mixed_word = mixed_word ^ lax.shift_right_logical(mixed_word, jnp.int32(15))
    mixed_word = mixed_word * jnp.int32(73244475)
    return mixed_word ^ lax.shift_right_logical(mixed_word, jnp.int32(16))


def sign_table(probe_seed, base, row_offset, col_offset, row_count, col_count, stride):
    row_ids = lax.broadcasted_iota(jnp.int32, (row_count, col_count), 0) + row_offset
    col_ids = lax.broadcasted_iota(jnp.int32, (row_count, col_count), 1) + col_offset
    index_table = base + row_ids * stride + col_ids
    word = mixing(mixing(probe_seed) ^ index_table)
    return (1 - 2 * (word & 1)).astype(jnp.bfloat16)


def lead_product(left, right):
    return lax.dot_general(left, right, LEADING, preferred_element_type=jnp.float32)


def shards(tokens, norm_gain, gate_weight, up_weight, down_weight, target, probe_seeds):
    local_width = gate_weight.shape[1]
    first_unit = lax.axis_index("tp") * local_width
    token_count = tokens.shape[1]
    probe_count = probe_seeds.shape[0]
    feature_rows = tokens.shape[0]
    widened = tokens.astype(jnp.float32)
    squares = jnp.sum(widened * widened, axis=0)
    total_squares = lax.psum(squares, "tp")
    inverse_rms = lax.rsqrt(total_squares / D + EPSILON)
    normed = (widened * inverse_rms[None, :] * norm_gain.astype(jnp.float32)[:, None]).astype(
        jnp.bfloat16
    )
    shard_piece = lax.all_gather(normed, "tp", axis=0, tiled=True)
    offset = jnp.int32(0)
    length = shard_piece.shape[0]
    result = [lead_product(gate_weight, shard_piece), lead_product(up_weight, shard_piece)]
    for project_probe_index in range(probe_count):
        probe_seed = probe_seeds[project_probe_index]
        gate_signs = sign_table(probe_seed, 0, offset, first_unit, length, local_width, FF)
        up_signs = sign_table(probe_seed, D * FF, offset, first_unit, length, local_width, FF)
        result.append(lead_product(gate_signs, shard_piece))
        result.append(lead_product(up_signs, shard_piece))
    sums = tuple(result)
    gate_pre = sums[0]
    up_pre = sums[1]
    gate_dots = [sums[2 + 2 * probe_index] * D ** (-0.5) for probe_index in range(probe_count)]
    up_dots = [sums[3 + 2 * probe_index] * D ** (-0.5) for probe_index in range(probe_count)]
    sigmoid_gate = jax.nn.sigmoid(gate_pre)
    activated = gate_pre * sigmoid_gate
    first_d = sigmoid_gate * (1.0 + gate_pre * (1.0 - sigmoid_gate))
    second_d = sigmoid_gate * (1.0 - sigmoid_gate) * (2.0 + gate_pre * (1.0 - 2.0 * sigmoid_gate))
    hidden = (activated * up_pre).astype(jnp.bfloat16)
    hidden_dots = [
        (first_d * gate_dots[probe_index] * up_pre + activated * up_dots[probe_index]).astype(
            jnp.bfloat16
        )
        for probe_index in range(probe_count)
    ]

    def forward_terms(offset, length, probe_list, with_primal):
        parts = []
        if with_primal:
            parts.append(lead_product(down_weight, hidden))
        for probe_index in probe_list:
            down_signs = sign_table(
                probe_seeds[probe_index], 2 * D * FF, first_unit, offset, local_width, length, D
            )
            parts.append(
                lead_product(down_weight, hidden_dots[probe_index])
                + lead_product(down_signs, hidden) * FF ** (-0.5)
            )
        return parts[0]

    probe_terms = []
    output_primal = lax.psum_scatter(
        forward_terms(
            jnp.int32(0), lax.axis_size("tp") * feature_rows, probe_list=(), with_primal=True
        ),
        "tp",
        scatter_dimension=0,
        tiled=True,
    )
    residual = output_primal - target.astype(jnp.float32)
    grad_out = (residual / token_count).astype(jnp.bfloat16)
    back = None
    for probe_index in range(probe_count):
        tangent_sum = lax.psum_scatter(
            forward_terms(
                jnp.int32(0),
                lax.axis_size("tp") * feature_rows,
                probe_list=(probe_index,),
                with_primal=False,
            ),
            "tp",
            scatter_dimension=0,
            tiled=True,
        )
        sent = jnp.concatenate([grad_out, tangent_sum.astype(jnp.bfloat16)], axis=1)
        with_back = probe_index == 0
        amount = 4 if with_back else 3
        totals = tuple((jnp.zeros((local_width, token_count), jnp.float32) for _ in range(amount)))
        accumulate_shard_piece = lax.all_gather(sent, "tp", axis=0, tiled=True)
        accumulate_offset = jnp.int32(0)
        accumulate_probe_list = (probe_index,)
        accumulate_length = accumulate_shard_piece.shape[0]
        grad_piece = accumulate_shard_piece[:, :token_count]
        accumulate_result = list(totals)
        start_slot = 0
        if with_back:
            accumulate_result[0] = jnp.dot(
                down_weight, grad_piece, preferred_element_type=jnp.float32
            )
            start_slot = 1
        for slot_index, accumulate_probe_index in enumerate(accumulate_probe_list):
            tangent_piece = accumulate_shard_piece[
                :, (slot_index + 1) * token_count : (slot_index + 2) * token_count
            ]
            accumulate_down_signs = sign_table(
                probe_seeds[accumulate_probe_index],
                2 * D * FF,
                first_unit,
                accumulate_offset,
                local_width,
                accumulate_length,
                D,
            )
            base_slot = start_slot + 3 * slot_index
            accumulate_result[base_slot] = jnp.dot(
                down_weight, tangent_piece, preferred_element_type=jnp.float32
            )
            accumulate_result[base_slot + 1] = jnp.dot(
                accumulate_down_signs, grad_piece, preferred_element_type=jnp.float32
            )
            accumulate_result[base_slot + 2] = jnp.dot(
                accumulate_down_signs, tangent_piece, preferred_element_type=jnp.float32
            )
        gathered = tuple(accumulate_result)
        if with_back:
            back = gathered[0]
        probe_terms.append(gathered[-3:])
    gate_trace = jnp.zeros((local_width,), jnp.float32)
    up_trace = jnp.zeros((local_width,), jnp.float32)
    down_trace = jnp.zeros((local_width,), jnp.float32)
    for probe_index in range(probe_count):
        down_tan, signed_grad, signed_tan = probe_terms[probe_index]
        cross = down_tan / token_count
        probe_grad = signed_grad * FF ** (-0.5)
        probe_tan = signed_tan * FF ** (-0.5) / token_count
        dd_hidden = cross + probe_grad
        gate_dot = gate_dots[probe_index]
        up_dot = up_dots[probe_index]
        dd_gate = (
            dd_hidden * up_pre * first_d
            + back * up_dot * first_d
            + back * up_pre * second_d * gate_dot
        )
        dd_up = dd_hidden * activated + back * first_d * gate_dot
        gate_trace = gate_trace + jnp.sum(gate_dot * dd_gate, axis=1)
        up_trace = up_trace + jnp.sum(up_dot * dd_up, axis=1)
        down_trace = down_trace + jnp.sum(
            hidden_dots[probe_index].astype(jnp.float32) * probe_grad
            + hidden.astype(jnp.float32) * probe_tan,
            axis=1,
        )
    return jnp.stack([gate_trace, up_trace, down_trace]) / probe_count


def solution(mesh):
    return jax.shard_map(
        shards,
        mesh=mesh,
        in_specs=(
            P("tp", "grp"),
            P("tp"),
            P(None, "tp"),
            P(None, "tp"),
            P("tp", None),
            P("tp", "grp"),
            P("grp"),
        ),
        out_specs=P("grp", "tp"),
        check_vma=False,
    )
```

profile of v0, /device:TPU:0, one launch (start us, length us, event | category | flops | bytes accessed | tf_op | source)
XLA Modules:
  0.0 741.9 jit_solution(15398878699868738577)
XLA Ops:
  6.5 0.0 all-gather.4.cloned.1.call-start
  6.5 1.0 fusion.134
  7.5 34.9 %psum.7 = f32[128]{0:T(128)S(1)} all-reduce(f32[128]{0:T(128)S(1)} %fusion.134), channel_id=1, replica_groups=mesh['grp'=2,'tp'=16] {'tp'}, use_global_device_ids=true, to_apply=%region_1.0 | all-reduce | flops 128 | bytes 1024 | tf_op jit(solution)/shard_map/psum | solution.py:42
  42.5 0.7 convert_element_type.62
  43.1 1.7 fusion.136
  44.8 0.0 all-gather.4.cloned.1.call-update
  44.9 0.0 reduce-scatter.8.cloned.1.call-start
  44.9 1.3 fusion.187
  48.8 0.6 multiply_add_fusion.2
  49.4 34.3 %all-gather.4.cloned.1.call-done = bf16[8192,128]{1,0:T(8,128)(2,1)} async-done(((bf16[512,128]{1,0:T(8,128)(2,1)}), bf16[8192,128]{1,0:T(8,128)(2,1)}) %all-gather.4.cloned.1.call-update) | async-done | bytes 2097168 | tf_op jit(solution)/shard_map/all_gather | solution.py:47
  83.7 31.6 %fusion.74 = f32[1792,128]{0,1:T(8,128)S(1)} fusion(bf16[8192,128]{1,0:T(8,128)(2,1)} %all-gather.4.cloned.1.call-done, s32[]{:T(128)S(6)} %xor.151, s32[1792]{0:T(1024)S(1)} %iota_add_fusion.1, s32[8192]{0:T(1024)S(1)} %iota_multiply_fusion), kind=kOutput, calls=%fused_computation.78 | convolution fusion | flops 3963846656 | bytes 3054596 | tf_op jit(solution)/shard_map/dot_general | solution.py:31
  115.3 0.0 copy-done
  115.3 0.0 copy-start.13
  115.3 30.3 %fusion.68 = f32[1792,128]{0,1:T(8,128)S(1)} fusion(bf16[8192,128]{1,0:T(8,128)(2,1)S(1)} %copy-done, s32[1792]{0:T(1024)S(1)} %iota_add_fusion.1, s32[8192]{0:T(1024)S(1)} %iota_multiply_fusion, s32[]{:T(128)S(6)} %xor.134), kind=kOutput, calls=%fused_computation.76 | convolution fusion | flops 3963846656 | bytes 3054596 | tf_op jit(solution)/shard_map/dot_general | solution.py:31
  145.6 0.0 copy-start.14
  145.6 30.8 %fusion.71 = f32[1792,128]{0,1:T(8,128)S(1)} fusion(bf16[8192,128]{1,0:T(8,128)(2,1)S(1)} %copy-done, s32[8192]{0:T(1024)S(1)} %broadcast_add_fusion, s32[1792]{0:T(1024)S(1)} %iota_add_fusion.1, s32[]{:T(128)S(6)} %xor.134), kind=kOutput, calls=%fused_computation.77 | convolution fusion | flops 3963846656 | bytes 3054596 | tf_op jit(solution)/shard_map/dot_general | solution.py:31
  176.4 0.0 copy-start.15
  176.4 11.9 %convolution_bitcast_fusion.4 = f32[1792,128]{0,1:T(8,128)S(1)} fusion(bf16[8192,128]{1,0:T(8,128)(2,1)S(1)} %copy-done, bf16[8192,1792]{1,0:T(8,128)(2,1)} %param.10), kind=kOutput, calls=%fused_computation.93 | convolution fusion | flops 3758096384 | bytes 32374784 | tf_op jit(solution)/shard_map/dot_general | solution.py:31
  188.3 11.9 %convolution_bitcast_fusion.5 = f32[1792,128]{0,1:T(8,128)S(1)} fusion(bf16[8192,128]{1,0:T(8,128)(2,1)S(1)} %copy-done, bf16[8192,1792]{1,0:T(8,128)(2,1)} %param.9), kind=kOutput, calls=%fused_computation.94 | convolution fusion | flops 3758096384 | bytes 32374784 | tf_op jit(solution)/shard_map/dot_general | solution.py:31
  200.2 0.0 copy-done.13
  200.2 0.0 copy-done.14
  200.2 0.0 copy-done.15
  200.2 0.0 copy-start.6
  200.2 31.8 %add_convert_fusion = (bf16[1792,128]{0,1:T(8,128)(2,1)S(1)}, bf16[1792,128]{0,1:T(8,128)(2,1)S(1)}, bf16[1792,128]{0,1:T(8,128)(2,1)S(1)}, f32[1792,128]{0,1:T(8,128)}) fusion(f32[1792,128]{0,1:T(8,128)S(1)} %convolution_bitcast_fusion.4, f32[1792,128]{0,1:T(8,128)S(1)} %fusion.74, f32[1792,128]{0,1:T(8,128)S(1)} %convolution_bitcast_fusion.5, ...), kind=kOutput, calls=%fused_computation.120 | convolution fusion | flops 3968434176 | bytes 9018372 | tf_op jit(solution)/shard_map/dot_general | solution.py:31
  232.0 0.0 copy-start.12
  232.1 0.8 copy-done.7
  232.8 11.5 %convolution_bitcast_fusion = f32[8192,128]{0,1:T(8,128)S(1)} fusion(bf16[1792,128]{0,1:T(8,128)(2,1)S(1)} %get-tuple-element.11, bf16[1792,8192]{1,0:T(8,128)(2,1)} %param.11), kind=kOutput, calls=%fused_computation.69 | convolution fusion | flops 3758096384 | bytes 34013184 | tf_op jit(solution)/shard_map/dot_general | solution.py:31
  244.4 0.0 copy-done.12
  244.4 33.6 %fusion.65 = f32[8192,128]{0,1:T(8,128)} fusion(f32[8192,128]{0,1:T(8,128)S(1)} %convolution_bitcast_fusion, bf16[1792,128]{0,1:T(8,128)(2,1)S(1)} %get-tuple-element.13, s32[]{:T(128)S(6)} %xor.151, s32[1792]{0:T(1024)S(1)} %copy-done.12), kind=kOutput, calls=%fused_computation.75 | convolution fusion | flops 3965714432 | bytes 8854532 | tf_op jit(solution)/shard_map/dot_general | solution.py:31
  277.9 0.0 reduce-scatter.8.cloned.1.call-update
  278.0 0.0 reduce-scatter.6.cloned.1.call-start
  278.0 12.3 %convolution_bitcast_fusion.1 = f32[8192,128]{0,1:T(8,128)S(1)} fusion(bf16[1792,128]{0,1:T(8,128)(2,1)S(1)} %get-tuple-element.12, bf16[1792,8192]{1,0:T(8,128)(2,1)} %param.11), kind=kOutput, calls=%fused_computation.70 | convolution fusion | flops 3758096384 | bytes 34013184 | tf_op jit(solution)/shard_map/dot_general | solution.py:31
  290.3 33.7 %fusion.59 = f32[8192,128]{0,1:T(8,128)} fusion(f32[8192,128]{0,1:T(8,128)S(1)} %convolution_bitcast_fusion.1, bf16[1792,128]{0,1:T(8,128)(2,1)S(1)} %get-tuple-element.13, s32[1792]{0:T(1024)S(1)} %copy-done.12, s32[]{:T(128)S(6)} %xor.134), kind=kOutput, calls=%fused_computation.73 | convolution fusion | flops 3965714432 | bytes 8854532 | tf_op jit(solution)/shard_map/dot_general | solution.py:31
  324.1 0.0 copy-start.11
  324.1 0.0 reduce-scatter.6.cloned.1.call-update
  324.1 0.0 reduce-scatter.4.cloned.1.call-start
  324.1 15.4 %convolution_bitcast_fusion.2 = f32[8192,128]{0,1:T(8,128)} fusion(bf16[1792,128]{0,1:T(8,128)(2,1)S(1)} %get-tuple-element.13, bf16[1792,8192]{1,0:T(8,128)(2,1)} %param.11), kind=kOutput, calls=%fused_computation.71 | convolution fusion | flops 3758096384 | bytes 34013184 | tf_op jit(solution)/shard_map/dot_general | solution.py:31
  339.6 0.0 reduce-scatter.4.cloned.1.call-update
  339.6 0.0 all-gather.6.cloned.1.call-start
  339.6 0.1 copy.8
  339.8 9.5 %reduce-scatter.8.cloned.1.call-done = f32[512,128]{0,1:T(8,128)} async-done(((f32[8192,128]{0,1:T(8,128)}), f32[512,128]{0,1:T(8,128)}) %reduce-scatter.8.cloned.1.call-update) | async-done | bytes 262160 | tf_op jit(solution)/shard_map/reduce_scatter | solution.py:101
  349.3 1.0 convert_element_type.75
  350.2 74.9 %reduce-scatter.6.cloned.1.call-done = f32[512,128]{0,1:T(8,128)} async-done(((f32[8192,128]{0,1:T(8,128)}), f32[512,128]{0,1:T(8,128)}) %reduce-scatter.6.cloned.1.call-update) | async-done | bytes 262160 | tf_op jit(solution)/shard_map/reduce_scatter | solution.py:101
  425.2 1.0 convert_element_type.70
  426.1 74.2 %reduce-scatter.4.cloned.1.call-done = f32[512,128]{0,1:T(8,128)} async-done(((f32[8192,128]{0,1:T(8,128)}), f32[512,128]{0,1:T(8,128)}) %reduce-scatter.4.cloned.1.call-update) | async-done | bytes 262160 | tf_op jit(solution)/shard_map/reduce_scatter | solution.py:89
  500.4 1.0 multiply_convert_fusion.1
  501.3 0.9 pad_maximum_fusion
  502.2 0.0 all-gather.6.cloned.1.call-update
  502.2 0.0 all-gather.8.cloned.1.call-start
  502.3 0.5 all-gather.8.cloned.1.call-update
  502.8 52.0 %all-gather.6.cloned.1.call-done = bf16[8192,256]{0,1:T(8,128)(2,1)} async-done(((bf16[512,256]{0,1:T(8,128)(2,1)}), bf16[8192,256]{0,1:T(8,128)(2,1)}) %all-gather.6.cloned.1.call-update) | async-done | bytes 4194320 | tf_op jit(solution)/shard_map/all_gather | solution.py:116
  554.8 32.9 %fusion.80 = f32[1792,128]{0,1:T(8,128)S(1)} fusion(s32[1792]{0:T(1024)S(1)} %copy-done.12, s32[]{:T(128)S(6)} %xor.134, bf16[8192,256]{0,1:T(8,128)(2,1)} %all-gather.6.cloned.1.call-done), kind=kOutput, calls=%fused_computation.80 | convolution fusion | flops 3963846656 | bytes 3021828 | tf_op jit(solution)/shard_map/dot_general | solution.py:145
  587.8 32.1 %fusion.120 = f32[1792]{0:T(1024)S(1)} fusion(bf16[8192,256]{0,1:T(8,128)(2,1)S(1)} %copy-done.1, s32[1792]{0:T(1024)S(1)} %copy-done.12, s32[]{:T(128)S(6)} %xor.134, bf16[1792,128]{0,1:T(8,128)(2,1)S(1)} %get-tuple-element.13, f32[1792,128]{0,1:T(8,128)S(1)} %fusion.80, bf16[1792,128]{0,1:T(8,128)(2,1)S(1)} %get-tuple-element.12), kind=kOutput, calls=%fused_computation.107 | convolution fusion | flops 3965221120 | bytes 3947524 | tf_op jit(solution)/shard_map/dot_general | solution.py:148
  619.9 0.0 all-gather.8.cloned.1.call-done
  619.9 0.0 copy-start.3
  619.9 0.0 copy-start.8
  619.9 0.0 copy-start.10
  620.0 33.0 %fusion.92 = f32[1792,128]{0,1:T(8,128)S(1)} fusion(s32[]{:T(128)S(6)} %xor.151, s32[1792]{0:T(1024)S(1)} %copy-done.12, bf16[8192,256]{0,1:T(8,128)(2,1)} %all-gather.8.cloned.1.call-done), kind=kOutput, calls=%fused_computation.84 | convolution fusion | flops 3963846656 | bytes 3021828 | tf_op jit(solution)/shard_map/dot_general | solution.py:145
  653.0 31.9 %fusion.115 = f32[1792]{0:T(1024)S(1)} fusion(bf16[8192,256]{0,1:T(8,128)(2,1)S(1)} %copy-done.3, s32[]{:T(128)S(6)} %xor.151, s32[1792]{0:T(1024)S(1)} %copy-done.12, bf16[1792,128]{0,1:T(8,128)(2,1)S(1)} %copy-done.10, f32[1792,128]{0,1:T(8,128)S(1)} %fusion.92, bf16[1792,128]{0,1:T(8,128)(2,1)S(1)} %copy-done.8), kind=kOutput, calls=%fused_computation.106 | convolution fusion | flops 3965221120 | bytes 3947524 | tf_op jit(solution)/shard_map/dot_general | solution.py:148
  684.9 15.3 %fusion.107 = f32[1792,128]{0,1:T(8,128)} fusion(f32[1792,128]{0,1:T(8,128)S(1)} %fusion.80, bf16[1792,8192]{1,0:T(8,128)(2,1)} %param.11, bf16[8192,256]{0,1:T(8,128)(2,1)S(1)} %copy-done.2), kind=kOutput, calls=%fused_computation.96 | convolution fusion | flops 3758555136 | bytes 33292288 | tf_op jit(solution)/shard_map/dot_general | solution.py:142
  700.2 15.3 %fusion.106 = f32[1792,128]{0,1:T(8,128)} fusion(f32[1792,128]{0,1:T(8,128)S(1)} %fusion.92, bf16[1792,8192]{1,0:T(8,128)(2,1)} %param.11, bf16[8192,256]{0,1:T(8,128)(2,1)S(1)} %copy-done.3), kind=kOutput, calls=%fused_computation.95 | convolution fusion | flops 3758555136 | bytes 33292288 | tf_op jit(solution)/shard_map/dot_general | solution.py:142
  715.5 18.0 %fusion.130 = (f32[1792]{0:T(1024)}, f32[1792]{0:T(1024)S(1)}, f32[1792]{0:T(1024)S(1)}, f32[1792]{0:T(1024)}) fusion(f32[1792,128]{0,1:T(8,128)} %copy-done.13, f32[1792,128]{0,1:T(8,128)} %get-tuple-element.18, f32[1792,128]{0,1:T(8,128)} %fusion.106, f32[1792,128]{0,1:T(8,128)S(1)} %copy-done.5, f32[1792,128]{0,1:T(8,128)} %copy-done.6, ...), kind=kOutput, calls=%fused_computation.114 | convolution fusion | flops 3767952384 | bytes 38825984 | tf_op jit(solution)/shard_map/dot_general | solution.py:124
  733.4 0.7 add.174
  734.2 0.6 maximum_multiply_fusion
  (26 shorter events, 0.1 us)
Async XLA Ops:
  6.5 77.2 %all-gather.4.cloned.1.call-start = ((), (), s32[]{:S(2)}) async-start(), calls=%async_computation.3 | async-start | bytes 2228224 | tf_op jit(solution)/shard_map/all_gather | solution.py:47
  44.9 304.4 %reduce-scatter.8.cloned.1.call-start = ((), (), s32[]{:S(2)}) async-start(), calls=%async_computation.7 | async-start | bytes 4456448 | tf_op jit(solution)/shard_map/reduce_scatter | solution.py:101
  83.7 31.6 %copy-start = (bf16[8192,128]{1,0:T(8,128)(2,1)S(1)}, bf16[8192,128]{1,0:T(8,128)(2,1)}, u32[]{:S(2)}) copy-start(bf16[8192,128]{1,0:T(8,128)(2,1)} %all-gather.4.cloned.1.call-done) | copy-start | bytes 6291460
  115.3 84.9 %copy-start.13 = (f32[1792,128]{0,1:T(8,128)}, f32[1792,128]{0,1:T(8,128)S(1)}, u32[]{:S(2)}) copy-start(f32[1792,128]{0,1:T(8,128)S(1)} %fusion.74) | copy-start | bytes 2752516
  145.6 54.6 %copy-start.14 = (f32[1792,128]{0,1:T(8,128)}, f32[1792,128]{0,1:T(8,128)S(1)}, u32[]{:S(2)}) copy-start(f32[1792,128]{0,1:T(8,128)S(1)} %fusion.68) | copy-start | bytes 2752516
  176.4 23.8 %copy-start.15 = (f32[1792,128]{0,1:T(8,128)}, f32[1792,128]{0,1:T(8,128)S(1)}, u32[]{:S(2)}) copy-start(f32[1792,128]{0,1:T(8,128)S(1)} %fusion.71) | copy-start | bytes 2752516
  188.3 43.7 %copy-start.4 = (f32[1792,128]{0,1:T(8,128)}, f32[1792,128]{0,1:T(8,128)S(1)}, u32[]{:S(2)}) copy-start(f32[1792,128]{0,1:T(8,128)S(1)} %convolution_bitcast_fusion.4) | copy-start | bytes 2752516
  200.2 31.8 %copy-start.6 = (f32[1792,128]{0,1:T(8,128)}, f32[1792,128]{0,1:T(8,128)S(1)}, u32[]{:S(2)}) copy-start(f32[1792,128]{0,1:T(8,128)S(1)} %convolution_bitcast_fusion.5) | copy-start | bytes 2752516
  232.0 0.8 copy-start.7
  232.0 355.7 %copy-start.9 = (bf16[1792,128]{0,1:T(8,128)(2,1)}, bf16[1792,128]{0,1:T(8,128)(2,1)S(1)}, u32[]{:S(2)}) copy-start(bf16[1792,128]{0,1:T(8,128)(2,1)S(1)} %get-tuple-element.13) | copy-start | bytes 1376260
  232.0 12.3 %copy-start.12 = (s32[1792]{0:T(1024)S(1)}, s32[1792]{0:T(1024)}, u32[]{:S(2)}) copy-start(s32[1792]{0:T(1024)} %multiply_add_fusion.2) | copy-start | bytes 21508
  278.0 147.2 %reduce-scatter.6.cloned.1.call-start = ((), (), s32[]{:S(2)}) async-start(), calls=%async_computation.5 | async-start | bytes 4456448 | tf_op jit(solution)/shard_map/reduce_scatter | solution.py:101
  324.1 15.6 %copy-start.11 = (bf16[512,128]{1,0:T(8,128)(2,1)S(1)}, bf16[512,128]{1,0:T(8,128)(2,1)}, u32[]{:S(2)}) copy-start(bf16[512,128]{1,0:T(8,128)(2,1)} %param.12) | copy-start | bytes 393220
  324.1 176.3 %reduce-scatter.4.cloned.1.call-start = ((), (), s32[]{:S(2)}) async-start(), calls=%async_computation.4 | async-start | bytes 4456448 | tf_op jit(solution)/shard_map/reduce_scatter | solution.py:89
  339.6 215.2 %all-gather.6.cloned.1.call-start = ((), (), s32[]{:S(2)}) async-start(), calls=%async_computation.6 | async-start | bytes 4456448 | tf_op jit(solution)/shard_map/all_gather | solution.py:116
  502.2 117.7 %all-gather.8.cloned.1.call-start = ((), (), s32[]{:S(2)}) async-start(), calls=%async_computation.8 | async-start | bytes 4456448 | tf_op jit(solution)/shard_map/all_gather | solution.py:116
  554.8 33.0 %copy-start.1 = (bf16[8192,256]{0,1:T(8,128)(2,1)S(1)}, bf16[8192,256]{0,1:T(8,128)(2,1)}, u32[]{:S(2)}) copy-start(bf16[8192,256]{0,1:T(8,128)(2,1)} %all-gather.6.cloned.1.call-done) | copy-start | bytes 12582916
  619.9 33.0 %copy-start.3 = (bf16[8192,256]{0,1:T(8,128)(2,1)S(1)}, bf16[8192,256]{0,1:T(8,128)(2,1)}, u32[]{:S(2)}) copy-start(bf16[8192,256]{0,1:T(8,128)(2,1)} %all-gather.8.cloned.1.call-done) | copy-start | bytes 12582916
  619.9 33.0 %copy-start.8 = (bf16[1792,128]{0,1:T(8,128)(2,1)S(1)}, bf16[1792,128]{0,1:T(8,128)(2,1)}, u32[]{:S(2)}) copy-start(bf16[1792,128]{0,1:T(8,128)(2,1)} %copy-done.7) | copy-start | bytes 1376260
  619.9 33.0 %copy-start.10 = (bf16[1792,128]{0,1:T(8,128)(2,1)S(1)}, bf16[1792,128]{0,1:T(8,128)(2,1)}, u32[]{:S(2)}) copy-start(bf16[1792,128]{0,1:T(8,128)(2,1)} %copy-done.9) | copy-start | bytes 1376260
  653.0 31.9 %copy-start.2 = (bf16[8192,256]{0,1:T(8,128)(2,1)S(1)}, bf16[8192,256]{0,1:T(8,128)(2,1)}, u32[]{:S(2)}) copy-start(bf16[8192,256]{0,1:T(8,128)(2,1)} %all-gather.6.cloned.1.call-done) | copy-start | bytes 12582916
  700.2 15.3 %copy-start.5 = (f32[1792,128]{0,1:T(8,128)S(1)}, f32[1792,128]{0,1:T(8,128)}, u32[]{:S(2)}) copy-start(f32[1792,128]{0,1:T(8,128)} %copy-done.4) | copy-start | bytes 2752516
Sparse Core Ops, SparseCore 0:
  45.0 38.6 all-gather.3
  278.1 71.1 reduce-scatter.7
  353.6 71.5 reduce-scatter.5
  428.9 71.4 reduce-scatter.3
  502.6 52.1 all-gather.5
  557.1 51.3 all-gather.7
where the time goes:
time: 751 us; the launch traced here: 742 us
  matrix products  433 us (58%)
  waiting for transfers between devices  246 us (33%)
  blocking collectives  34.9 us (5%)
  between operations  16.6 us (2%)
  other arithmetic  9.15 us (1%)
    dot_general x11, matrix products, lead_product(): lax.dot_general(left, right, LEADING, preferred_element_type=jnp.float32)  255 us
    reduce_scatter x3, waiting for transfers between devices, shards(): lax.psum_scatter(forward_terms(jnp.int32(0), lax.axis_size('tp') * featur...  159 us
    dot_general x2, matrix products, shards(): jnp.dot(accumulate_down_signs, grad_piece, preferred_element_type=jnp.flo...  65.9 us
    dot_general x2, matrix products, shards(): jnp.dot(accumulate_down_signs, tangent_piece, preferred_element_type=jnp....  64 us
    all_gather x2, waiting for transfers between devices, shards(): accumulate_shard_piece = lax.all_gather(sent, 'tp', axis=0, tiled=True)  52 us
    psum x1, blocking collectives, shards(): total_squares = lax.psum(squares, 'tp')  34.9 us
    all_gather x1, waiting for transfers between devices, shards(): shard_piece = lax.all_gather(normed, 'tp', axis=0, tiled=True)  34.3 us
    dot_general x2, matrix products, shards(): jnp.dot(down_weight, tangent_piece, preferred_element_type=jnp.float32)  30.5 us
  transfers between devices with their start and end apart: 6, of which 5 were waited for; matrix products, arithmetic and copies ran while one was open for 18% of the time, Pallas kernels for 0%

commit v1 on v0

v1 whole, which is shorter than its diff:
```python
import functools
import math

import jax
import jax.numpy as jnp
from jax import lax
from jax.experimental import pallas as pl
from jax.experimental.pallas import tpu as pltpu
from jax.sharding import PartitionSpec as P

EPSILON = 1e-05
MIX = 73244475
VMEM_BYTES = 60 * 1024 * 1024


def wrap32(value):
    value &= 0xFFFFFFFF
    return value - (1 << 32) if value >= 1 << 31 else value


LAST_MIX = wrap32((MIX + (1 << 16)) << 15)


def mixing(word):
    word = word ^ lax.shift_right_logical(word, jnp.int32(16))
    word = word * jnp.int32(MIX)
    word = word ^ lax.shift_right_logical(word, jnp.int32(15))
    word = word * jnp.int32(MIX)
    return word ^ lax.shift_right_logical(word, jnp.int32(16))


def sign_tile(seed, base, row0, col0, rows, cols, row_stride, col_stride):
    sub = lax.broadcasted_iota(jnp.int32, (8, 128), 0)
    lane = lax.broadcasted_iota(jnp.int32, (8, 128), 1)
    groups = []
    for group in range(cols // 128):
        index = (
            base
            + (row0 + sub) * row_stride
            + (col0 + group * 128 + lane) * col_stride
        )
        word = seed ^ index
        word = word ^ lax.shift_right_logical(word, jnp.int32(16))
        pieces = [word * jnp.int32(MIX)]
        bit = 8
        while bit < rows:
            flips = [bit * row_stride]
            if flips[0] >= 1 << 16:
                flips.append(flips[0] >> 16)
            delta = None
            for flip in flips:
                plus, minus = jnp.int32(wrap32(MIX * flip)), jnp.int32(wrap32(-MIX * flip))
                term = jnp.where((word & jnp.int32(flip)) != 0, minus, plus)
                delta = term if delta is None else delta + term
            pieces = pieces + [piece + delta for piece in pieces]
            bit *= 2
        signs = []
        for piece in pieces:
            piece = piece ^ lax.shift_right_logical(piece, jnp.int32(15))
            piece = piece * jnp.int32(LAST_MIX)
            signs.append(jnp.where(piece < 0, jnp.float32(-1.0), jnp.float32(1.0)))
        groups.append(jnp.concatenate(signs, axis=0).astype(jnp.bfloat16))
    return jnp.concatenate(groups, axis=1)


def each_block(width, block, body):
    if block % 128 == 0:
        lax.fori_loop(
            0, width // block, lambda i, c: (body(pl.multiple_of(i * block, block)), c)[1], 0
        )
    else:
        for i in range(width // block):
            body(i * block)


def dotf(left, right):
    return jnp.dot(left, right, preferred_element_type=jnp.float32)


def project_kernel(
    model, hidden_units, block, probes,
    scalars, normed_t, normed, gate, up, gate_t, up_t, dots,
):
    step = pl.program_id(0)
    depth, width = gate.shape
    first = scalars[probes]

    @pl.when(step == 0)
    def _():
        gate_t[...] = jnp.zeros_like(gate_t)
        up_t[...] = jnp.zeros_like(up_t)
        dots[...] = jnp.zeros_like(dots)

    aligned = block % 128 == 0
    if not aligned:
        gate_t[...] += dotf(normed_t[...], gate[...])
        up_t[...] += dotf(normed_t[...], up[...])

    def body(start):
        cols = pl.ds(start, block)
        if aligned:
            gate_t[:, cols] += dotf(normed_t[...], gate[:, cols])
            up_t[:, cols] += dotf(normed_t[...], up[:, cols])
        for probe in range(probes):
            for table in range(2):
                tile = sign_tile(
                    scalars[probe], table * model * hidden_units, first + start,
                    step * depth, block, depth, 1, hidden_units,
                )
                dots[2 * probe + table, cols, :] += dotf(tile, normed[...])

    each_block(width, block, body)


def project(scalars, normed_t, normed, gate_weight, up_weight, block, probes, hidden_units):
    model, width = gate_weight.shape
    tokens = normed.shape[1]
    depth = 512
    whole = lambda *shape: pl.BlockSpec(shape, lambda i: (0,) * len(shape))
    rows = lambda cols: pl.BlockSpec((depth, cols), lambda i: (i, 0))
    return pl.pallas_call(
        functools.partial(project_kernel, model, hidden_units, block, probes),
        grid=(model // depth,),
        in_specs=[
            pl.BlockSpec(memory_space=pltpu.SMEM),
            pl.BlockSpec((tokens, depth), lambda i: (0, i)),
            rows(tokens),
            rows(width),
            rows(width),
        ],
        out_specs=[
            whole(tokens, width),
            whole(tokens, width),
            whole(2 * probes, width, tokens),
        ],
        out_shape=[
            jax.ShapeDtypeStruct((tokens, width), jnp.float32),
            jax.ShapeDtypeStruct((tokens, width), jnp.float32),
            jax.ShapeDtypeStruct((2 * probes, width, tokens), jnp.float32),
        ],
        compiler_params=pltpu.CompilerParams(vmem_limit_bytes=VMEM_BYTES),
        cost_estimate=pl.CostEstimate(
            flops=2 * 6 * model * width * tokens * 4,
            bytes_accessed=4 * model * width,
            transcendentals=0,
        ),
        name="project",
    )(scalars, normed_t, normed, gate_weight, up_weight)


def forward_kernel(
    model, hidden_units, block, probe, count, scalars, hidden_t, dot_t, down, out
):
    step = pl.program_id(0)
    width, depth = down.shape
    first = scalars[count]
    out[...] = jnp.zeros_like(out)

    def body(start):
        cols = pl.ds(start, block)
        tile = sign_tile(
            scalars[probe], 2 * model * hidden_units, first + start, step * depth,
            block, depth, model, 1,
        )
        out[...] += dotf(hidden_t[:, cols], tile)

    each_block(width, block, body)
    out[...] = out[...] * hidden_units ** (-0.5) + dotf(dot_t[...], down[...])


def forward(scalars, hidden_t, dot_t, down_weight, block, probe, count, hidden_units):
    width, model = down_weight.shape
    tokens = hidden_t.shape[0]
    depth = 512
    return pl.pallas_call(
        functools.partial(forward_kernel, model, hidden_units, block, probe, count),
        grid=(model // depth,),
        in_specs=[
            pl.BlockSpec(memory_space=pltpu.SMEM),
            pl.BlockSpec((tokens, width), lambda i: (0, 0)),
            pl.BlockSpec((tokens, width), lambda i: (0, 0)),
            pl.BlockSpec((width, depth), lambda i: (0, i)),
        ],
        out_specs=pl.BlockSpec((tokens, depth), lambda i: (0, i)),
        out_shape=jax.ShapeDtypeStruct((tokens, model), jnp.float32),
        compiler_params=pltpu.CompilerParams(vmem_limit_bytes=VMEM_BYTES),
        cost_estimate=pl.CostEstimate(
            flops=2 * 3 * model * width * tokens * 4,
            bytes_accessed=2 * model * width,
            transcendentals=0,
        ),
        name="forward_tangent",
    )(scalars, hidden_t, dot_t, down_weight)


def backward_kernel(
    model, hidden_units, block, probe, count, skip, scalars, grads, down, plain, signed
):
    step = pl.program_id(0)
    width, depth = down.shape
    first = scalars[count]

    @pl.when(step == 0)
    def _():
        plain[...] = jnp.zeros_like(plain)
        signed[...] = jnp.zeros_like(signed)

    def body(start):
        rows = pl.ds(start, block)
        tile = sign_tile(
            scalars[probe], 2 * model * hidden_units, first + start, step * depth,
            block, depth, model, 1,
        )
        plain[rows, :] += dotf(down[rows, :], grads[:, skip:])
        signed[rows, :] += dotf(tile, grads[...])

    each_block(width, block, body)


def backward(scalars, grads, down_weight, block, probe, count, skip, hidden_units):
    width, model = down_weight.shape
    columns = grads.shape[1]
    depth = 512
    return pl.pallas_call(
        functools.partial(backward_kernel, model, hidden_units, block, probe, count, skip),
        grid=(model // depth,),
        in_specs=[
            pl.BlockSpec(memory_space=pltpu.SMEM),
            pl.BlockSpec((depth, columns), lambda i: (i, 0)),
            pl.BlockSpec((width, depth), lambda i: (0, i)),
        ],
        out_specs=[
            pl.BlockSpec((width, columns - skip), lambda i: (0, 0)),
            pl.BlockSpec((width, columns), lambda i: (0, 0)),
        ],
        out_shape=[
            jax.ShapeDtypeStruct((width, columns - skip), jnp.float32),
            jax.ShapeDtypeStruct((width, columns), jnp.float32),
        ],
        compiler_params=pltpu.CompilerParams(vmem_limit_bytes=VMEM_BYTES),
        cost_estimate=pl.CostEstimate(
            flops=2 * 2 * model * width * columns * 2,
            bytes_accessed=2 * model * width,
            transcendentals=0,
        ),
        name="backward",
    )(scalars, grads, down_weight)


def shards(tokens, norm_gain, gate_weight, up_weight, down_weight, target, probe_seeds):
    model, width = gate_weight.shape
    devices = lax.axis_size("tp")
    hidden_units = width * devices
    first_unit = lax.axis_index("tp") * width
    count = tokens.shape[1]
    probes = probe_seeds.shape[0]
    block = math.gcd(width, 256)
    block = block & -block
    scalars = jnp.concatenate([mixing(probe_seeds), first_unit[None].astype(jnp.int32)])

    gathered = lax.all_gather(tokens, "tp", axis=0, tiled=True)
    gain = lax.all_gather(norm_gain, "tp", axis=0, tiled=True)
    widened = gathered.astype(jnp.float32)
    total_squares = jnp.sum(widened * widened, axis=0)
    inverse_rms = lax.rsqrt(total_squares / model + EPSILON)
    normed = (widened * inverse_rms[None, :] * gain.astype(jnp.float32)[:, None]).astype(
        jnp.bfloat16
    )
    gate_t, up_t, dots = project(
        scalars, normed.T, normed, gate_weight, up_weight, block, probes, hidden_units
    )
    gate_pre, up_pre = gate_t.T, up_t.T
    gate_dots = [dots[2 * probe] * model ** (-0.5) for probe in range(probes)]
    up_dots = [dots[2 * probe + 1] * model ** (-0.5) for probe in range(probes)]
    sigmoid_gate = jax.nn.sigmoid(gate_pre)
    activated = gate_pre * sigmoid_gate
    first_d = sigmoid_gate * (1.0 + gate_pre * (1.0 - sigmoid_gate))
    second_d = sigmoid_gate * (1.0 - sigmoid_gate) * (2.0 + gate_pre * (1.0 - 2.0 * sigmoid_gate))
    hidden = (activated * up_pre).astype(jnp.bfloat16)
    hidden_dots = [
        (first_d * gate_dots[p] * up_pre + activated * up_dots[p]).astype(jnp.bfloat16)
        for p in range(probes)
    ]
    hidden_t = hidden.T

    def scatter(value):
        return lax.psum_scatter(value, "tp", scatter_dimension=1, tiled=True)

    output = scatter(dotf(hidden_t, down_weight))
    tangents = [
        scatter(
            forward(
                scalars, hidden_t, hidden_dots[p].T, down_weight, block, p, probes, hidden_units
            )
        )
        for p in range(probes)
    ]
    grad_out = ((output.T - target.astype(jnp.float32)) / count).astype(jnp.bfloat16)
    grad_all = lax.all_gather(grad_out, "tp", axis=0, tiled=True)
    back = None
    gate_trace = up_trace = down_trace = jnp.zeros((width,), jnp.float32)
    for p in range(probes):
        tangent_all = lax.all_gather(
            tangents[p].T.astype(jnp.bfloat16), "tp", axis=0, tiled=True
        )
        skip = count if p else 0
        plain, signed = backward(
            scalars, jnp.concatenate([grad_all, tangent_all], axis=1), down_weight,
            block, p, probes, skip, hidden_units,
        )
        if p == 0:
            back = plain[:, :count]
        cross = plain[:, plain.shape[1] - count :] / count
        probe_grad = signed[:, :count] * hidden_units ** (-0.5)
        probe_tan = signed[:, count:] * hidden_units ** (-0.5) / count
        dd_hidden = cross + probe_grad
        gate_dot, up_dot = gate_dots[p], up_dots[p]
        dd_gate = (
            dd_hidden * up_pre * first_d
            + back * up_dot * first_d
            + back * up_pre * second_d * gate_dot
        )
        dd_up = dd_hidden * activated + back * first_d * gate_dot
        gate_trace = gate_trace + jnp.sum(gate_dot * dd_gate, axis=1)
        up_trace = up_trace + jnp.sum(up_dot * dd_up, axis=1)
        down_trace = down_trace + jnp.sum(
            hidden_dots[p].astype(jnp.float32) * probe_grad
            + hidden.astype(jnp.float32) * probe_tan,
            axis=1,
        )
    return jnp.stack([gate_trace, up_trace, down_trace]) / probes


def solution(mesh):
    return jax.shard_map(
        shards,
        mesh=mesh,
        in_specs=(
            P("tp", "grp"),
            P("tp"),
            P(None, "tp"),
            P(None, "tp"),
            P("tp", None),
            P("tp", "grp"),
            P("grp"),
        ),
        out_specs=P("grp", "tp"),
        check_vma=False,
    )
```

time: 751 us -> 666 us (0.89); the launches traced: 742 us -> 666 us
  matrix products: 433 us -> 17.6 us
  Pallas kernels: 0 us -> 258 us
  waiting for transfers between devices: 246 us -> 299 us
  other arithmetic: 9.15 us -> 34.1 us
  local copies, waits for them, and re-layouts: 2.27 us -> 20 us
  blocking collectives: 34.9 us -> 23.1 us
    dot_general x18 -> x1, matrix products: 433 us -> 17.6 us  [dotf(): return jnp.dot(left, right, preferred_element_type=jnp.float32)]
    pallas_call x0 -> x5, Pallas kernels: none -> 258 us  [the longest x1 90.2 us: project(): pl.pallas_call(functools.partial(project_kernel, model, hidden_units, blo...]
    all_gather x3 -> x4, waiting for transfers between devices: 86.3 us -> 147 us  [the longest x2 83.4 us: shards(): lax.all_gather(tangents[p].T.astype(jnp.bfloat16), 'tp', axis=0, tiled=True)]
    psum x1 -> x0, blocking collectives: 34.9 us -> none  [shards(): total_squares = lax.psum(squares, 'tp')]
    all_gather x0 -> x1, blocking collectives: none -> 23.1 us  [shards(): gain = lax.all_gather(norm_gain, 'tp', axis=0, tiled=True)]
    pallas_call x0 -> x4, local copies, waits for them, and re-layouts: none -> 13 us  [the longest x2 11.2 us: forward(): pl.pallas_call(functools.partial(forward_kernel, model, hidden_units, blo...]
    convert_element_type x5 -> x7, other arithmetic: 5.3 us -> 15.2 us  [the longest x1 4.34 us: shards(): (widened * inverse_rms[None, :] * gain.astype(jnp.float32)[:, None]).asty...]
  transfers between devices with their start and end apart: 6 -> 7, of which waited for: 5 -> 7; matrix products, arithmetic and copies ran while one was open for 18% -> 5% of each run, Pallas kernels for 0% -> 7%
where the time goes in v1:
time: 666 us
  waiting for transfers between devices  299 us (45%)
  Pallas kernels  258 us (39%)
  other arithmetic  34.1 us (5%)
  blocking collectives  23.1 us (3%)
  local copies, waits for them, and re-layouts  20 us (3%)
  matrix products  17.6 us (3%)
  between operations  13.6 us (2%)
    reduce_scatter x3, waiting for transfers between devices, scatter(): return lax.psum_scatter(value, 'tp', scatter_dimension=1, tiled=True)  151 us
    pallas_call x1, Pallas kernels, project(): pl.pallas_call(functools.partial(project_kernel, model, hidden_units, blo...  90.2 us
    pallas_call x2, Pallas kernels, forward(): pl.pallas_call(functools.partial(forward_kernel, model, hidden_units, blo...  86.8 us
    all_gather x2, waiting for transfers between devices, shards(): lax.all_gather(tangents[p].T.astype(jnp.bfloat16), 'tp', axis=0, tiled=True)  83.4 us
    pallas_call x2, Pallas kernels, backward(): pl.pallas_call(functools.partial(backward_kernel, model, hidden_units, bl...  80.7 us
    all_gather x1, waiting for transfers between devices, shards(): grad_all = lax.all_gather(grad_out, 'tp', axis=0, tiled=True)  42.6 us
    all_gather x1, blocking collectives, shards(): gain = lax.all_gather(norm_gain, 'tp', axis=0, tiled=True)  23.1 us
    all_gather x1, waiting for transfers between devices, shards(): gathered = lax.all_gather(tokens, 'tp', axis=0, tiled=True)  21.2 us
  transfers between devices with their start and end apart: 7, of which 7 were waited for; matrix products, arithmetic and copies ran while one was open for 5% of the time, Pallas kernels for 7%

profile of v1, /device:TPU:0, one launch (start us, length us, event | category | flops | bytes accessed | tf_op | source)
XLA Modules:
  0.0 665.8 jit_solution(15473898786621535643)
XLA Ops:
  6.5 0.0 all-gather.6.cloned.1.call-start
  6.5 0.7 all-gather.6.cloned.1.call-update
  7.3 0.0 reduce-scatter.8.cloned.1.call-start
  7.3 0.7 reshape.50
  8.0 23.1 %all-gather = bf16[16,1,512]{2,1,0:T(2,128)(2,1)S(1)} all-gather(bf16[1,1,512]{2,1,0:T(2,128)(2,1)S(1)} %reshape.50), channel_id=1, replica_groups=mesh['grp'=2,'tp'=16] {'tp'}, dimensions={0}, use_global_device_ids=true | all-gather | bytes 17408 | tf_op jit(solution)/shard_map/all_gather | solution.py:262
  31.2 0.7 shift-right-logical_xor_fusion
  31.8 0.6 pad_add_fusion.scalars
  32.4 21.2 %all-gather.6.cloned.1.call-done = bf16[8192,128]{1,0:T(8,128)(2,1)} async-done(((bf16[512,128]{1,0:T(8,128)(2,1)}), bf16[8192,128]{1,0:T(8,128)(2,1)}) %all-gather.6.cloned.1.call-update) | async-done | bytes 2097168 | tf_op jit(solution)/shard_map/all_gather | solution.py:261
  53.7 2.7 fusion
  56.4 0.0 copy-start
  56.4 3.6 fusion.42
  59.9 4.1 copy.16.normed_t
  64.0 0.0 copy-done
  64.0 4.3 fusion.2.normed
  68.4 90.2 %project.1 = (f32[128,1792]{1,0:T(8,128)}, f32[128,1792]{1,0:T(8,128)}, f32[4,1792,128]{2,1,0:T(8,128)}) custom-call(s32[3]{0:T(128)} %pad_add_fusion.scalars, bf16[128,8192]{1,0:T(8,128)(2,1)} %copy.16.normed_t, bf16[8192,128]{1,0:T(8,128)(2,1)} %fusion.2.normed, bf16[8192,1792]{1,0:T(8,128)(2,1)} %gate.1, bf16[8192,1792]{1,0:T(8,128)(2,1)} %up.1), custom_call_target="tpu_custom_call" | custom-call | flops 90194313216 | bytes 58720256 | tf_op jit(solution)/shard_map/project/pallas_call | solution.py:121
  158.6 0.0 copy-start.6
  158.6 1.5 copy.17
  160.2 0.0 copy-start.2
  160.2 2.8 multiply_convert_fusion.hidden_t
  163.0 0.0 copy-done.6
  163.0 0.3 copy.18
  163.3 0.0 copy-start.3
  163.3 3.1 fusion.12
  166.4 0.0 copy-done.2
  166.4 0.0 copy-start.4
  166.5 0.0 copy-start.5
  166.5 1.1 copy.22.dot_t
  167.5 43.4 %forward_tangent.3 = f32[128,8192]{1,0:T(8,128)} custom-call(s32[3]{0:T(128)} %pad_add_fusion.scalars, bf16[128,1792]{1,0:T(8,128)(2,1)} %multiply_convert_fusion.hidden_t, bf16[128,1792]{1,0:T(8,128)(2,1)} %copy.22.dot_t, bf16[1792,8192]{1,0:T(8,128)(2,1)} %down.7), custom_call_target="tpu_custom_call" | custom-call | flops 45097156608 | bytes 29360128 | tf_op jit(solution)/shard_map/forward_tangent/pallas_call | solution.py:175
  210.9 0.0 copy-done.3
  210.9 0.0 copy-done.4
  211.0 5.6 copy.23
  216.5 0.0 reduce-scatter.8.cloned.1.call-update
  216.6 0.0 reduce-scatter.6.cloned.1.call-start
  216.6 0.0 copy-done.5
  216.6 1.0 copy.20.dot_t
  217.6 43.4 %forward_tangent.2 = f32[128,8192]{1,0:T(8,128)} custom-call(s32[3]{0:T(128)} %pad_add_fusion.scalars, bf16[128,1792]{1,0:T(8,128)(2,1)} %multiply_convert_fusion.hidden_t, bf16[128,1792]{1,0:T(8,128)(2,1)} %copy.20.dot_t, bf16[1792,8192]{1,0:T(8,128)(2,1)} %down.7), custom_call_target="tpu_custom_call" | custom-call | flops 45097156608 | bytes 29360128 | tf_op jit(solution)/shard_map/forward_tangent/pallas_call | solution.py:175
  261.0 5.6 copy.21
  266.7 0.0 reduce-scatter.6.cloned.1.call-update
  266.7 0.2 reduce-scatter.4.cloned.1.call-start
  266.9 17.6 %fusion.39 = f32[128,8192]{0,1:T(8,128)} fusion(bf16[1792,128]{1,0:T(8,128)(2,1)S(1)} %get-tuple-element.32, bf16[1792,8192]{1,0:T(8,128)(2,1)} %down.7), kind=kOutput, calls=%fused_computation.86 | convolution fusion | flops 3758096384 | bytes 34013184 | tf_op jit(solution)/shard_map/dot_general | solution.py:77
  284.5 0.0 copy-start.7
  284.5 0.0 reduce-scatter.4.cloned.1.call-update
  284.5 0.0 all-gather.12.cloned.1.call-start
  284.6 3.6 reduce-scatter.8.cloned.1.call-done
  288.2 1.6 convert_bitcast_fusion
  289.8 0.0 all-gather.12.cloned.1.call-update
  289.8 0.0 all-gather.10.cloned.1.call-start
  289.9 74.0 %reduce-scatter.6.cloned.1.call-done = f32[128,512]{0,1:T(8,128)} async-done(((f32[128,8192]{0,1:T(8,128)}), f32[128,512]{0,1:T(8,128)}) %reduce-scatter.6.cloned.1.call-update) | async-done | bytes 262160 | tf_op jit(solution)/shard_map/reduce_scatter | solution.py:287
  363.9 1.6 convert_bitcast_fusion.1
  365.5 0.0 all-gather.10.cloned.1.call-update
  365.5 0.0 all-gather.8.cloned.1.call-start
  365.6 73.6 %reduce-scatter.4.cloned.1.call-done = f32[128,512]{0,1:T(8,128)} async-done(((f32[128,8192]{0,1:T(8,128)}), f32[128,512]{0,1:T(8,128)}) %reduce-scatter.4.cloned.1.call-update) | async-done | bytes 262160 | tf_op jit(solution)/shard_map/reduce_scatter | solution.py:287
  439.1 0.0 copy-done.7
  439.1 1.6 fusion.36
  440.8 0.0 all-gather.8.cloned.1.call-update
  440.8 40.9 %all-gather.12.cloned.1.call-done = bf16[8192,128]{1,0:T(8,128)(2,1)} async-done(((bf16[512,128]{1,0:T(8,128)(2,1)}), bf16[8192,128]{1,0:T(8,128)(2,1)}) %all-gather.12.cloned.1.call-update) | async-done | bytes 2097168 | tf_op jit(solution)/shard_map/all_gather | solution.py:303
  481.7 42.4 %all-gather.10.cloned.1.call-done = bf16[8192,128]{1,0:T(8,128)(2,1)} async-done(((bf16[512,128]{1,0:T(8,128)(2,1)}), bf16[8192,128]{1,0:T(8,128)(2,1)}) %all-gather.10.cloned.1.call-update) | async-done | bytes 2097168 | tf_op jit(solution)/shard_map/all_gather | solution.py:303
  524.2 42.6 %all-gather.8.cloned.1.call-done = bf16[8192,128]{1,0:T(8,128)(2,1)} async-done(((bf16[512,128]{1,0:T(8,128)(2,1)}), bf16[8192,128]{1,0:T(8,128)(2,1)}) %all-gather.8.cloned.1.call-update) | async-done | bytes 2097168 | tf_op jit(solution)/shard_map/all_gather | solution.py:299
  566.8 5.5 pad_maximum_fusion
  572.2 40.6 %backward.3 = (f32[1792,128]{1,0:T(8,128)}, f32[1792,256]{1,0:T(8,128)}) custom-call(s32[3]{0:T(128)} %pad_add_fusion.scalars, bf16[8192,256]{1,0:T(8,128)(2,1)} %get-tuple-element.30.grads, bf16[1792,8192]{1,0:T(8,128)(2,1)} %down.7), custom_call_target="tpu_custom_call" | custom-call | flops 30064771072 | bytes 29360128 | tf_op jit(solution)/shard_map/backward/pallas_call | solution.py:224
  612.9 40.1 %backward.2 = (f32[1792,256]{1,0:T(8,128)}, f32[1792,256]{1,0:T(8,128)}) custom-call(s32[3]{0:T(128)} %pad_add_fusion.scalars, bf16[8192,256]{1,0:T(8,128)(2,1)} %get-tuple-element.31.grads, bf16[1792,8192]{1,0:T(8,128)(2,1)} %down.7), custom_call_target="tpu_custom_call" | custom-call | flops 30064771072 | bytes 29360128 | tf_op jit(solution)/shard_map/backward/pallas_call | solution.py:224
  653.0 0.0 copy-done.1
  653.0 5.2 fusion.17
  658.3 0.6 maximum_multiply_fusion
  (9 shorter events, 0.1 us)
Async XLA Ops:
  6.5 47.1 %all-gather.6.cloned.1.call-start = ((), (), s32[]{:S(2)}) async-start(), calls=%async_computation.3 | async-start | bytes 2228224 | tf_op jit(solution)/shard_map/all_gather | solution.py:261
  7.3 280.9 %reduce-scatter.8.cloned.1.call-start = ((), (), s32[]{:S(2)}) async-start(), calls=%async_computation.8 | async-start | bytes 4456448 | tf_op jit(solution)/shard_map/reduce_scatter | solution.py:287
  56.4 7.7 %copy-start = (bf16[8192,128]{1,0:T(8,128)(2,1)S(1)}, bf16[8192,128]{1,0:T(8,128)(2,1)}, u32[]{:S(2)}) copy-start(bf16[8192,128]{1,0:T(8,128)(2,1)} %all-gather.6.cloned.1.call-done) | copy-start | bytes 6291460
  158.6 4.4 copy-start.6
  160.2 6.3 copy-start.2
  163.3 47.7 %copy-start.3 = (f32[128,1792]{0,1:T(8,128)}, f32[128,1792]{0,1:T(8,128)S(1)}, u32[]{:S(2)}) copy-start(f32[128,1792]{0,1:T(8,128)S(1)} %copy.18) | copy-start | bytes 2752516
  166.4 44.5 %copy-start.4 = (bf16[1792,128]{1,0:T(8,128)(2,1)}, bf16[1792,128]{1,0:T(8,128)(2,1)S(1)}, u32[]{:S(2)}) copy-start(bf16[1792,128]{1,0:T(8,128)(2,1)S(1)} %get-tuple-element.28) | copy-start | bytes 1376260
  166.5 50.2 %copy-start.5 = (bf16[1792,128]{1,0:T(8,128)(2,1)}, bf16[1792,128]{1,0:T(8,128)(2,1)S(1)}, u32[]{:S(2)}) copy-start(bf16[1792,128]{1,0:T(8,128)(2,1)S(1)} %get-tuple-element.29) | copy-start | bytes 1376260
  216.6 147.3 %reduce-scatter.6.cloned.1.call-start = ((), (), s32[]{:S(2)}) async-start(), calls=%async_computation.6 | async-start | bytes 4456448 | tf_op jit(solution)/shard_map/reduce_scatter | solution.py:287
  266.7 172.5 %reduce-scatter.4.cloned.1.call-start = ((), (), s32[]{:S(2)}) async-start(), calls=%async_computation.4 | async-start | bytes 4456448 | tf_op jit(solution)/shard_map/reduce_scatter | solution.py:287
  284.5 154.6 %copy-start.7 = (bf16[512,128]{1,0:T(8,128)(2,1)S(1)}, bf16[512,128]{1,0:T(8,128)(2,1)}, u32[]{:S(2)}) copy-start(bf16[512,128]{1,0:T(8,128)(2,1)} %param.12) | copy-start | bytes 393220
  284.5 197.2 %all-gather.12.cloned.1.call-start = ((), (), s32[]{:S(2)}) async-start(), calls=%async_computation.9 | async-start | bytes 2228224 | tf_op jit(solution)/shard_map/all_gather | solution.py:303
  289.8 234.4 %all-gather.10.cloned.1.call-start = ((), (), s32[]{:S(2)}) async-start(), calls=%async_computation.7 | async-start | bytes 2228224 | tf_op jit(solution)/shard_map/all_gather | solution.py:303
  365.5 201.2 %all-gather.8.cloned.1.call-start = ((), (), s32[]{:S(2)}) async-start(), calls=%async_computation.5 | async-start | bytes 2228224 | tf_op jit(solution)/shard_map/all_gather | solution.py:299
  612.9 40.1 %copy-start.1 = (f32[4,1792,128]{2,1,0:T(8,128)S(1)}, f32[4,1792,128]{2,1,0:T(8,128)}, u32[]{:S(2)}) copy-start(f32[4,1792,128]{2,1,0:T(8,128)} %get-tuple-element.12) | copy-start | bytes 11010052
Sparse Core Ops, SparseCore 0:
  9.5 44.0 all-gather.5
  216.7 71.4 reduce-scatter.7
  292.5 71.3 reduce-scatter.5
  367.6 71.4 reduce-scatter.3
  441.4 40.3 all-gather.11
  484.0 40.1 all-gather.9
  526.6 40.1 all-gather.7

commit v2 on v1

--- a/solution.py
+++ b/solution.py
@@ -162,10 +162,10 @@
             scalars[probe], 2 * model * hidden_units, first + start, step * depth,
             block, depth, model, 1,
         )
-        out[...] += dotf(hidden_t[:, cols], tile)
+        out[...] += dotf(hidden_t[:, cols], tile)[None]
 
     each_block(width, block, body)
-    out[...] = out[...] * hidden_units ** (-0.5) + dotf(dot_t[...], down[...])
+    out[...] = out[...] * hidden_units ** (-0.5) + dotf(dot_t[...], down[...])[None]
 
 
 def forward(scalars, hidden_t, dot_t, down_weight, block, probe, count, hidden_units):
@@ -181,8 +181,8 @@
             pl.BlockSpec((tokens, width), lambda i: (0, 0)),
             pl.BlockSpec((width, depth), lambda i: (0, i)),
         ],
-        out_specs=pl.BlockSpec((tokens, depth), lambda i: (0, i)),
-        out_shape=jax.ShapeDtypeStruct((tokens, model), jnp.float32),
+        out_specs=pl.BlockSpec((1, tokens, depth), lambda i: (i, 0, 0)),
+        out_shape=jax.ShapeDtypeStruct((model // depth, tokens, depth), jnp.float32),
         compiler_params=pltpu.CompilerParams(vmem_limit_bytes=VMEM_BYTES),
         cost_estimate=pl.CostEstimate(
             flops=2 * 3 * model * width * tokens * 4,
@@ -194,11 +194,12 @@
 
 
 def backward_kernel(
-    model, hidden_units, block, probe, count, skip, scalars, grads, down, plain, signed
+    model, hidden_units, block, probe, count, skip, scalars, grad, tangent, down, plain, signed
 ):
     step = pl.program_id(0)
     width, depth = down.shape
     first = scalars[count]
+    grads = jnp.concatenate([grad[...], tangent[...]], axis=1)
 
     @pl.when(step == 0)
     def _():
@@ -212,21 +213,22 @@
             block, depth, model, 1,
         )
         plain[rows, :] += dotf(down[rows, :], grads[:, skip:])
-        signed[rows, :] += dotf(tile, grads[...])
+        signed[rows, :] += dotf(tile, grads)
 
     each_block(width, block, body)
 
 
-def backward(scalars, grads, down_weight, block, probe, count, skip, hidden_units):
+def backward(scalars, grad, tangent, down_weight, block, probe, count, skip, hidden_units):
     width, model = down_weight.shape
-    columns = grads.shape[1]
+    columns = 2 * grad.shape[1]
     depth = 512
     return pl.pallas_call(
         functools.partial(backward_kernel, model, hidden_units, block, probe, count, skip),
         grid=(model // depth,),
         in_specs=[
             pl.BlockSpec(memory_space=pltpu.SMEM),
-            pl.BlockSpec((depth, columns), lambda i: (i, 0)),
+            pl.BlockSpec((depth, columns // 2), lambda i: (i, 0)),
+            pl.BlockSpec((depth, columns // 2), lambda i: (i, 0)),
             pl.BlockSpec((width, depth), lambda i: (0, i)),
         ],
         out_specs=[
@@ -244,7 +246,7 @@
             transcendentals=0,
         ),
         name="backward",
-    )(scalars, grads, down_weight)
+    )(scalars, grad, tangent, down_weight)
 
 
 def shards(tokens, norm_gain, gate_weight, up_weight, down_weight, target, probe_seeds):
@@ -258,8 +260,12 @@
     block = block & -block
     scalars = jnp.concatenate([mixing(probe_seeds), first_unit[None].astype(jnp.int32)])
 
-    gathered = lax.all_gather(tokens, "tp", axis=0, tiled=True)
-    gain = lax.all_gather(norm_gain, "tp", axis=0, tiled=True)
+    features = tokens.shape[0]
+    gain_rows = -(-features // count)
+    padded = jnp.pad(norm_gain, (0, gain_rows * count - features)).reshape(gain_rows, count)
+    joined = lax.all_gather(jnp.concatenate([tokens, padded], axis=0), "tp", axis=0)
+    gathered = joined[:, :features].reshape(model, count)
+    gain = joined[:, features:].reshape(devices, gain_rows * count)[:, :features].reshape(model)
     widened = gathered.astype(jnp.float32)
     total_squares = jnp.sum(widened * widened, axis=0)
     inverse_rms = lax.rsqrt(total_squares / model + EPSILON)
@@ -283,29 +289,50 @@
     ]
     hidden_t = hidden.T
 
+    chips = devices // 2
+    core = lax.axis_index("tp") % 2
+    swap = [(i, i ^ 1) for i in range(devices)]
+    across = [[2 * i + c for i in range(chips)] for c in range(2)]
+
     def scatter(value):
-        return lax.psum_scatter(value, "tp", scatter_dimension=1, tiled=True)
-
-    output = scatter(dotf(hidden_t, down_weight))
-    tangents = [
-        scatter(
-            forward(
-                scalars, hidden_t, hidden_dots[p].T, down_weight, block, p, probes, hidden_units
+        if value.shape[0] == devices:
+            pairs = value.reshape(chips, 2, count, features)
+        else:
+            wide = jnp.transpose(value, (1, 0, 2)).reshape(count, chips, 2, features)
+            pairs = jnp.transpose(wide, (1, 2, 0, 3))
+        mine = lax.dynamic_index_in_dim(pairs, core, 1, keepdims=False)
+        other = lax.dynamic_index_in_dim(pairs, 1 - core, 1, keepdims=False)
+        sent = (mine + lax.ppermute(other, "tp", swap)).astype(jnp.bfloat16)
+        arrived = lax.all_to_all(sent, "tp", 0, 0, axis_index_groups=across, tiled=True)
+        return jnp.sum(arrived.astype(jnp.float32), axis=0).T
+
+    primal = dotf(hidden_t, down_weight)
+    primal, hidden_t, first_dot = lax.optimization_barrier(
+        (primal, hidden_t, hidden_dots[0].T)
+    )
+    output = lax.psum_scatter(primal, "tp", scatter_dimension=1, tiled=True)
+    tangents = []
+    dot_t = first_dot
+    for p in range(probes):
+        tangent = scatter(
+            forward(scalars, hidden_t, dot_t, down_weight, block, p, probes, hidden_units)
+        ).astype(jnp.bfloat16)
+        if p + 1 < probes:
+            tangent, dot_t, hidden_t = lax.optimization_barrier(
+                (tangent, hidden_dots[p + 1].T, hidden_t)
             )
-        )
-        for p in range(probes)
-    ]
+        tangents.append(tangent)
     grad_out = ((output.T - target.astype(jnp.float32)) / count).astype(jnp.bfloat16)
     grad_all = lax.all_gather(grad_out, "tp", axis=0, tiled=True)
+    tangents_all = [lax.all_gather(t, "tp", axis=0, tiled=True) for t in tangents[:-1]]
+    tangents_all[0], tangents[-1] = lax.optimization_barrier((tangents_all[0], tangents[-1]))
+    tangents_all.append(lax.all_gather(tangents[-1], "tp", axis=0, tiled=True))
     back = None
     gate_trace = up_trace = down_trace = jnp.zeros((width,), jnp.float32)
     for p in range(probes):
-        tangent_all = lax.all_gather(
-            tangents[p].T.astype(jnp.bfloat16), "tp", axis=0, tiled=True
-        )
         skip = count if p else 0
         plain, signed = backward(
-            scalars, jnp.concatenate([grad_all, tangent_all], axis=1), down_weight,
+            scalars, grad_all, tangents_all[p], down_weight,
             block, p, probes, skip, hidden_units,
         )
         if p == 0:

time: 666 us -> 466 us (0.70)
  waiting for transfers between devices: 299 us -> 53.4 us
  blocking collectives: 23.1 us -> 77.8 us
  other arithmetic: 34.1 us -> 26.2 us
    reduce_scatter x3 -> x1, waiting for transfers between devices: 151 us -> 0.01 us  [shards(): output = lax.psum_scatter(primal, 'tp', scatter_dimension=1, tiled=True)]
    all_to_all x0 -> x2, blocking collectives: none -> 77.8 us  [scatter(): lax.all_to_all(sent, 'tp', 0, 0, axis_index_groups=across, tiled=True)]
    all_gather x3, waiting for transfers between devices: 105 us -> 46.4 us  [the longest x1 44.2 us: shards(): lax.all_gather(jnp.concatenate([tokens, padded], axis=0), 'tp', axis=0)]
    all_gather x1, waiting for transfers between devices: 42.6 us -> 0.02 us  [shards(): grad_all = lax.all_gather(grad_out, 'tp', axis=0, tiled=True)]
    all_gather x1 -> x0, blocking collectives: 23.1 us -> none  [shards(): gain = lax.all_gather(norm_gain, 'tp', axis=0, tiled=True)]
    pallas_call x2 -> x0, local copies, waits for them, and re-layouts: 11.2 us -> none  [forward(): pl.pallas_call(functools.partial(forward_kernel, model, hidden_units, blo...]
    optimization_barrier x0 -> x3, local copies, waits for them, and re-layouts: none -> 7.56 us  [the longest x2 6.57 us: shards(): lax.optimization_barrier((primal, hidden_t, hidden_dots[0].T))]
    ppermute x0 -> x2, waiting for transfers between devices: none -> 6.93 us  [scatter(): sent = (mine + lax.ppermute(other, 'tp', swap)).astype(jnp.bfloat16)]
  transfers between devices with their start and end apart: 7 -> 7, of which waited for: 7 -> 4; matrix products, arithmetic and copies ran while one was open for 5% -> 4% of each run, Pallas kernels for 7% -> 27%
where the time goes in v2:
time: 466 us; the launch traced here: 465 us
  Pallas kernels  257 us (55%)
  blocking collectives  77.8 us (17%)
  waiting for transfers between devices  53.4 us (11%)
  other arithmetic  26.2 us (6%)
  local copies, waits for them, and re-layouts  21.1 us (5%)
  matrix products  16 us (3%)
  between operations  13.4 us (3%)
    pallas_call x1, Pallas kernels, project(): pl.pallas_call(functools.partial(project_kernel, model, hidden_units, blo...  90.4 us
    pallas_call x2, Pallas kernels, forward(): pl.pallas_call(functools.partial(forward_kernel, model, hidden_units, blo...  86.8 us
    pallas_call x2, Pallas kernels, backward(): pl.pallas_call(functools.partial(backward_kernel, model, hidden_units, bl...  79.6 us
    all_to_all x2, blocking collectives, scatter(): lax.all_to_all(sent, 'tp', 0, 0, axis_index_groups=across, tiled=True)  77.8 us
    all_gather x1, waiting for transfers between devices, shards(): lax.all_gather(jnp.concatenate([tokens, padded], axis=0), 'tp', axis=0)  44.2 us
    dot_general x1, matrix products, dotf(): return jnp.dot(left, right, preferred_element_type=jnp.float32)  16 us
  transfers between devices with their start and end apart: 7, of which 4 were waited for; matrix products, arithmetic and copies ran while one was open for 4% of the time, Pallas kernels for 27%

profile of v2, /device:TPU:0, one launch (start us, length us, event | category | flops | bytes accessed | tf_op | source)
XLA Modules:
  0.0 465.1 jit_solution(18295240645645704721)
XLA Ops:
  6.5 0.0 all-gather.13.cloned.1.call-start
  6.5 1.6 maximum_bitcast_fusion
  8.1 0.0 all-gather.13.cloned.1.call-update
  8.1 0.0 reduce-scatter.2.cloned.1.call-start
  8.2 0.7 shift-right-logical_xor_fusion
  8.9 0.6 pad_add_fusion.scalars
  9.5 44.2 %all-gather.13.cloned.1.call-done = bf16[16,516,128]{2,1,0:T(8,128)(2,1)} async-done(((bf16[1,516,128]{2,1,0:T(8,128)(2,1)}), bf16[16,516,128]{2,1,0:T(8,128)(2,1)}) %all-gather.13.cloned.1.call-update) | async-done | bytes 2113552 | tf_op jit(solution)/shard_map/all_gather | solution.py:266
  53.7 2.8 multiply_reduce_fusion
  56.6 0.8 slice.49
  57.4 0.0 copy-done.2
  57.4 0.4 slice_convert_fusion
  57.8 3.5 fusion.1.normed
  61.3 0.0 copy-start.1
  61.3 3.0 copy.14.normed_t
  64.3 0.0 copy-done.1
  64.3 90.4 %project.1 = (f32[128,1792]{1,0:T(8,128)}, f32[128,1792]{1,0:T(8,128)}, f32[4,1792,128]{2,1,0:T(8,128)}) custom-call(s32[3]{0:T(128)} %pad_add_fusion.scalars, bf16[128,8192]{1,0:T(8,128)(2,1)} %copy.14.normed_t, bf16[8192,128]{1,0:T(8,128)(2,1)} %copy-done.1, bf16[8192,1792]{1,0:T(8,128)(2,1)} %gate.1, bf16[8192,1792]{1,0:T(8,128)(2,1)} %up.1), custom_call_target="tpu_custom_call" | custom-call | flops 90194313216 | bytes 58720256 | tf_op jit(solution)/shard_map/project/pallas_call | solution.py:121
  154.6 1.6 copy.15
  156.2 0.0 copy-start.3
  156.2 0.0 copy-done.9
  156.3 0.1 copy-done.10
  156.4 1.0 multiply_convert_fusion.hidden_t
  157.4 0.3 copy.16
  157.7 0.0 copy-start.4
  157.7 3.1 fusion.13
  160.8 0.0 copy-done.3
  160.8 0.0 copy-done.4
  160.9 0.0 copy-start.5
  160.9 0.0 copy-start.8
  160.9 0.0 copy-start.7
  160.9 16.0 %fusion.40 = f32[128,8192]{1,0:T(8,128)} fusion(bf16[1792,128]{1,0:T(8,128)(2,1)S(1)} %get-tuple-element.46, bf16[1792,8192]{1,0:T(8,128)(2,1)} %down.7), kind=kOutput, calls=%fused_computation.89 | convolution fusion | flops 3758096384 | bytes 34013184 | tf_op jit(solution)/shard_map/dot_general | solution.py:77
  176.9 5.6 %copy.17 = f32[128,8192]{0,1:T(8,128)} copy(f32[128,8192]{1,0:T(8,128)} %fusion.40) | data formatting | bytes 8388608 | tf_op jit(solution)/shard_map/optimization_barrier | solution.py:310
  182.5 0.0 reduce-scatter.2.cloned.1.call-update
  182.5 0.0 all-gather.9.cloned.1.call-start
  182.5 1.0 copy.18.dot_t
  183.5 43.4 %forward_tangent.2 = f32[16,128,512]{2,1,0:T(8,128)} custom-call(s32[3]{0:T(128)} %pad_add_fusion.scalars, bf16[128,1792]{1,0:T(8,128)(2,1)} %multiply_convert_fusion.hidden_t, bf16[128,1792]{1,0:T(8,128)(2,1)} %copy.18.dot_t, bf16[1792,8192]{1,0:T(8,128)(2,1)} %down.7), custom_call_target="tpu_custom_call" | custom-call | flops 45097156608 | bytes 29360128 | tf_op jit(solution)/shard_map/forward_tangent/pallas_call | solution.py:175
  227.0 3.1 dynamic-slice_bitcast_fusion.1
  230.1 0.2 collective-permute-start
  230.3 4.3 collective-permute-done
  234.6 2.6 fusion.3
  237.2 36.3 %all_to_all.10 = bf16[8,128,512]{2,1,0:T(8,128)(2,1)S(1)} all-to-all(bf16[8,128,512]{2,1,0:T(8,128)(2,1)S(1)} %fusion.3), channel_id=1, replica_groups={{0,2,4,6,8,10,12,14},{1,3,5,7,9,11,13,15},{16,18,20,22,24,26,28,30},{17..., dimensions={0} | all-to-all | bytes 2097152 | tf_op jit(solution)/shard_map/all_to_all | solution.py:306
  273.5 0.1 reduce_sum.88
  273.7 0.8 copy.19
  274.5 1.0 copy.20.dot_t
  275.4 0.0 all-gather.9.cloned.1.call-update
  275.5 0.0 all-gather.7.cloned.1.call-start
  275.5 43.4 %forward_tangent.3 = f32[16,128,512]{2,1,0:T(8,128)} custom-call(s32[3]{0:T(128)} %pad_add_fusion.scalars, bf16[128,1792]{1,0:T(8,128)(2,1)} %multiply_convert_fusion.hidden_t, bf16[128,1792]{1,0:T(8,128)(2,1)} %copy.20.dot_t, bf16[1792,8192]{1,0:T(8,128)(2,1)} %down.7), custom_call_target="tpu_custom_call" | custom-call | flops 45097156608 | bytes 29360128 | tf_op jit(solution)/shard_map/forward_tangent/pallas_call | solution.py:175
  319.0 3.1 dynamic-slice_bitcast_fusion
  322.1 0.0 collective-permute-start.1
  322.1 0.0 copy-done.11
  322.1 1.6 fusion.37
  323.7 0.0 all-gather.7.cloned.1.call-update
  323.8 0.0 all-gather.11.cloned.1.call-start
  323.8 2.6 collective-permute-done.1
  326.5 1.9 fusion.2
  328.4 41.4 %all_to_all.11 = bf16[8,128,512]{2,1,0:T(8,128)(2,1)S(1)} all-to-all(bf16[8,128,512]{2,1,0:T(8,128)(2,1)S(1)} %fusion.2), channel_id=1, replica_groups={{0,2,4,6,8,10,12,14},{1,3,5,7,9,11,13,15},{16,18,20,22,24,26,28,30},{17..., dimensions={0} | all-to-all | bytes 2097152 | tf_op jit(solution)/shard_map/all_to_all | solution.py:306
  369.8 0.1 reduce_sum.89
  370.0 0.8 copy.21
  370.8 0.0 all-gather.11.cloned.1.call-update
  370.8 0.0 all-gather.7.cloned.1.call-done.grad
  370.8 40.4 %backward.2 = (f32[1792,256]{1,0:T(8,128)}, f32[1792,256]{1,0:T(8,128)}) custom-call(s32[3]{0:T(128)} %pad_add_fusion.scalars, bf16[8192,128]{1,0:T(8,128)(2,1)} %all-gather.7.cloned.1.call-done.grad, bf16[8192,128]{1,0:T(8,128)(2,1)} %all-gather.9.cloned.1.call-done.tangent, bf16[1792,8192]{1,0:T(8,128)(2,1)} %down.7), custom_call_target="tpu_custom_call" | custom-call | flops 30064771072 | bytes 29360128 | tf_op jit(solution)/shard_map/backward/pallas_call | solution.py:225
  411.2 2.1 all-gather.11.cloned.1.call-done.tangent
  413.3 39.2 %backward.3 = (f32[1792,128]{1,0:T(8,128)}, f32[1792,256]{1,0:T(8,128)}) custom-call(s32[3]{0:T(128)} %pad_add_fusion.scalars, bf16[8192,128]{1,0:T(8,128)(2,1)} %all-gather.7.cloned.1.call-done.grad, bf16[8192,128]{1,0:T(8,128)(2,1)} %all-gather.11.cloned.1.call-done.tangent, bf16[1792,8192]{1,0:T(8,128)(2,1)} %down.7), custom_call_target="tpu_custom_call" | custom-call | flops 30064771072 | bytes 29360128 | tf_op jit(solution)/shard_map/backward/pallas_call | solution.py:225
  452.5 5.3 %fusion.18 = (f32[1792]{0:T(1024)S(1)}, f32[1792]{0:T(1024)S(1)}, f32[1792]{0:T(1024)S(1)}, f32[1792]{0:T(1024)S(1)}, f32[1792]{0:T(1024)S(1)}, /*index=5*/f32[1792]{0:T(1024)S(1)}) fusion(f32[128,1792]{0,1:T(8,128)} %copy-done.4, f32[128,1792]{0,1:T(8,128)} %copy-done.3, f32[1792,256]{1,0:T(8,128)} %get-tuple-element.30, f32[4,1792,128]{2,1,0:T(8,128)S(1)} %copy-done, ...), kind=kLoop, calls=%fused_computation.32 | loop fusion | flops 15128064 | bytes 13346816 | tf_op jit(solution)/shard_map/reduce_sum | solution.py:351
  457.9 0.6 maximum_multiply_fusion
  (21 shorter events, 0.1 us)
Async XLA Ops:
  6.5 47.2 %all-gather.13.cloned.1.call-start = ((), (), s32[]{:S(2)}) async-start(), calls=%async_computation.7 | async-start | bytes 2263040 | tf_op jit(solution)/shard_map/all_gather | solution.py:266
  8.1 313.9 %reduce-scatter.2.cloned.1.call-start = ((), (), s32[]{:S(2)}) async-start(), calls=%async_computation.3 | async-start | bytes 4456448 | tf_op jit(solution)/shard_map/reduce_scatter | solution.py:313
  53.7 3.6 copy-start.2
  61.3 3.0 copy-start.1
  154.6 1.6 copy-start.9
  154.6 1.7 copy-start.10
  156.2 4.6 copy-start.3
  157.7 3.2 copy-start.4
  160.9 16.0 %copy-start.5 = (bf16[1792,128]{1,0:T(8,128)(2,1)}, bf16[1792,128]{1,0:T(8,128)(2,1)S(1)}, u32[]{:S(2)}) copy-start(bf16[1792,128]{1,0:T(8,128)(2,1)S(1)} %get-tuple-element.46) | copy-start | bytes 1376260
  160.9 21.7 %copy-start.8 = (bf16[1792,128]{1,0:T(8,128)(2,1)}, bf16[1792,128]{1,0:T(8,128)(2,1)S(1)}, u32[]{:S(2)}) copy-start(bf16[1792,128]{1,0:T(8,128)(2,1)S(1)} %get-tuple-element.45) | copy-start | bytes 1376260
  160.9 113.6 %copy-start.7 = (bf16[1792,128]{1,0:T(8,128)(2,1)}, bf16[1792,128]{1,0:T(8,128)(2,1)S(1)}, u32[]{:S(2)}) copy-start(bf16[1792,128]{1,0:T(8,128)(2,1)S(1)} %get-tuple-element.44) | copy-start | bytes 1376260
  182.5 188.3 %all-gather.9.cloned.1.call-start = ((), (), s32[]{:S(2)}) async-start(), calls=%async_computation.5 | async-start | bytes 2228224 | tf_op jit(solution)/shard_map/all_gather | solution.py:327
  230.1 4.5 collective-permute-start
  275.5 95.3 %all-gather.7.cloned.1.call-start = ((), (), s32[]{:S(2)}) async-start(), calls=%async_computation.4 | async-start | bytes 2228224 | tf_op jit(solution)/shard_map/all_gather | solution.py:326
  319.0 3.1 copy-start.11
  322.1 4.4 collective-permute-start.1
  323.8 89.5 %all-gather.11.cloned.1.call-start = ((), (), s32[]{:S(2)}) async-start(), calls=%async_computation.6 | async-start | bytes 2228224 | tf_op jit(solution)/shard_map/all_gather | solution.py:329
  411.2 41.4 %copy-start.6 = (bf16[1792,128]{1,0:T(8,128)(2,1)S(1)}, bf16[1792,128]{1,0:T(8,128)(2,1)}, u32[]{:S(2)}) copy-start(bf16[1792,128]{1,0:T(8,128)(2,1)} %copy-done.5) | copy-start | bytes 1376260
  413.3 39.2 %copy-start = (f32[4,1792,128]{2,1,0:T(8,128)S(1)}, f32[4,1792,128]{2,1,0:T(8,128)}, u32[]{:S(2)}) copy-start(f32[4,1792,128]{2,1,0:T(8,128)} %get-tuple-element.20) | copy-start | bytes 11010052
Sparse Core Ops, SparseCore 0:
  9.5 44.1 all-gather.12
  182.6 78.9 reduce-scatter.1
  275.6 40.4 all-gather.8
  323.9 46.8 all-gather.6
  373.0 40.2 all-gather.10
